TPU v7x, 32 devices: a whole 2x2x4 slice. The times are simulated.
32 devices in a mesh: groups: 2 (over y), seq: 8 (over z, x), tp: 2 (over core).
Axes of the slice: x: 2, y: 2, z: 4, core: 2. Of those that a mesh axis runs over, the one named last changes fastest.
Arguments:
- query_rows: bfloat16 [2048, 4096], P(('groups', 'seq'), 'tp'), parts along dimension 0, may hold values from -1.78125 to 1.78125
- key_rows: bfloat16 [2048, 4096], P(('groups', 'seq'), 'tp'), parts along dimension 0, may hold values from -1.78125 to 1.78125
- value_rows: bfloat16 [2048, 4096], P(('groups', 'seq'), 'tp'), parts along dimension 0, may hold values from -180 to 180
- log_decay: float32 [32, 2048], P('tp', ('groups', 'seq')), parts along dimension 1, may hold values from -2 to 0
- carried_state: bfloat16 [64, 128, 128], P(('groups', 'tp')), parts along dimension 0, may hold values from -48 to 48
- norm_gain: float32 [4096], P('tp'), may hold values from 0.1 to 1.9
Outputs:
- attention_out: bfloat16 [2048, 4096], P(('groups', 'seq'), 'tp'), parts along dimension 0
There are 2 independent parts, one for each index of `groups`. A program takes and returns all parts, laid end to end along the dimension named above; an argument that names none is the same for every part. Nothing has to cross between parts.
All inputs are finite; a program needn't handle non-finite values.
Results may differ from a plain program's by a relative error of at most 0.007.
Values may be sent and summed in bfloat16 or wider, within the bound.
A program may use at most 256 MiB of HBM per device.

v0:
```python
import jax
import jax.numpy as jnp
from jax import lax
from jax.sharding import PartitionSpec as P


def prefix(x, axis, combine, identity):
    size, here = (lax.axis_size(axis), lax.axis_index(axis))
    everything = jax.tree.map(
        lambda part, kind: lax.all_gather(part.astype(kind), axis), x, (jnp.bfloat16, jnp.bfloat16)
    )
    start = jax.tree.map(
        lambda part, zero: jnp.broadcast_to(jnp.asarray(zero, part.dtype), part.shape), x, identity
    )

    def step(k, before):
        reached = k < here
        new = combine(
            before, jax.tree.map(lambda part, own: part[k].astype(own.dtype), everything, x)
        )
        return jax.tree.map(lambda a, b: jnp.where(reached, a, b), new, before)

    return lax.fori_loop(0, size, step, start)


def block_local(query_block, key_block, value_block, decay_block):
    head_count, row_count = decay_block.shape
    head_width = query_block.shape[1] // head_count
    query_heads = query_block.reshape(row_count, head_count, head_width)
    key_heads = key_block.reshape(row_count, head_count, head_width)
    value_heads = value_block.reshape(row_count, head_count, head_width)
    cumulative = jnp.cumsum(decay_block, axis=1)
    scores = jnp.einsum("thd,shd->hts", query_heads, key_heads, preferred_element_type=jnp.float32)
    causal = jnp.tril(jnp.ones((row_count, row_count), dtype=bool))[None]
    spread = cumulative[:, :, None] - cumulative[:, None, :]
    weights = jnp.where(causal, jnp.exp(jnp.minimum(spread, 0.0)), 0.0)
    mixing = (scores * weights).astype(jnp.bfloat16)
    inside = jnp.einsum("hts,shd->thd", mixing, value_heads, preferred_element_type=jnp.float32)
    block_log = cumulative[:, -1]
    key_decayed = (
        key_heads.astype(jnp.float32) * jnp.exp(block_log[:, None] - cumulative).T[:, :, None]
    ).astype(jnp.bfloat16)
    block_state = jnp.einsum(
        "thd,the->hde", key_decayed, value_heads, preferred_element_type=jnp.float32
    ).astype(jnp.bfloat16)
    query_decayed = (query_heads.astype(jnp.float32) * jnp.exp(cumulative).T[:, :, None]).astype(
        jnp.bfloat16
    )
    return (inside, query_decayed, block_state, block_log)


def joined(earlier, later):
    return (earlier[0] + later[0], jnp.exp(later[0])[:, None, None] * earlier[1] + later[1])


def per_device(query_rows, key_rows, value_rows, log_decay, carried_state, norm_gain):
    inside, query_decayed, block_state, block_log = block_local(
        query_rows, key_rows, value_rows, log_decay
    )
    starting = (jnp.zeros_like(block_log), jnp.zeros(block_state.shape, jnp.float32))
    prefix_log, prefix_state = prefix(
        (block_log, block_state.astype(jnp.float32)), "seq", joined, starting
    )
    entering = (
        jnp.exp(prefix_log)[:, None, None] * carried_state.astype(jnp.float32) + prefix_state
    ).astype(jnp.bfloat16)
    outside = jnp.einsum(
        "thd,hde->the", query_decayed, entering, preferred_element_type=jnp.float32
    )
    combined = (inside + outside).reshape(query_rows.shape[0], query_rows.shape[1])
    square_total = lax.psum(jnp.sum(combined * combined, axis=1), "tp")
    meansq = square_total / (combined.shape[1] * lax.axis_size("tp"))
    return (combined * lax.rsqrt(meansq + 1e-06)[:, None] * norm_gain[None]).astype(jnp.bfloat16)


def solution(mesh):
    in_specs = (
        P(("groups", "seq"), "tp"),
        P(("groups", "seq"), "tp"),
        P(("groups", "seq"), "tp"),
        P("tp", ("groups", "seq")),
        P(("groups", "tp"), None, None),
        P("tp"),
    )
    out_specs = P(("groups", "seq"), "tp")
    return jax.shard_map(
        per_device, mesh=mesh, in_specs=in_specs, out_specs=out_specs, check_vma=False
    )
```

profile of v0, /device:TPU:0, one launch (start us, length us, event | category | flops | bytes accessed | tf_op | source)
XLA Modules:
  0.0 111.4 jit_solution(1179798817656269207)
XLA Ops:
  6.5 0.0 copy-start
  6.5 0.0 all-gather.4.cloned.1.call-start
  6.5 1.0 reduce_window_sum.11
  7.6 0.2 slice_reduce_fusion
  7.8 0.1 exponential_bitcast_fusion
  7.8 1.3 %copy.28 = bf16[128,2048]{0,1:T(8,128)(2,1)S(1)} copy(bf16[128,2048]{1,0:T(8,128)(2,1)} %param.9) | data formatting | bytes 1048576 | tf_op jit(solution)/shard_map/reshape | solution.py:30
  9.2 2.2 %convolution_convert_fusion = bf16[16,128,128]{2,1,0:T(8,128)(2,1)} fusion(bf16[128,16,128]{0,2,1:T(8,128)(2,1)S(1)} %bitcast.57, f32[128,16]{0,1:T(8,128)S(1)} %get-tuple-element.153, bf16[128,2048]{1,0:T(8,128)(2,1)} %param.10), kind=kOutput, calls=%fused_computation.10 | convolution fusion | flops 68157440 | bytes 1581056 | tf_op jit(solution)/shard_map/thd,the->hde/dot_general | solution.py:43
  11.3 0.0 all-gather.4.cloned.1.call-update
  11.4 1.3 %dynamic-slice = u32[1]{0:T(128)} dynamic-slice(u32[32]{0:T(128)} %constant.47, u32[]{:T(128)S(6)} %add.54), dynamic_slice_sizes={1} | dynamic-slice | bytes 12
  13.2 0.2 fusion.24
  13.4 0.2 dynamic-update-slice
  13.7 23.4 %all-reduce = bf16[128]{0:T(256)(128)(2,1)S(1)} all-reduce(bf16[128]{0:T(256)(128)(2,1)S(1)} %dynamic-update-slice), channel_id=2, replica_groups=mesh['groups'=2,'seq'=8,'tp'=2] {'seq'}, use_global_device_ids=true, to_apply=%add | all-reduce | flops 128 | bytes 512
  37.1 0.1 reshape.55
  37.2 0.0 copy-done
  37.2 2.8 %convolution_bitcast_fusion.1 = f32[128,16,128]{0,2,1:T(8,128)} fusion(bf16[128,16,128]{0,2,1:T(8,128)(2,1)S(1)} %bitcast.58, f32[16,128]{1,0:T(8,128)S(1)} %reduce_window_sum.11, pred[128,128]{1,0:T(8,128)(4,1)S(1)} %iota_compare_fusion, bf16[128,2048]{1,0:T(8,128)(2,1)} %param.10, bf16[128,2048]{1,0:T(8,128)(2,1)S(1)} %copy-done), kind=kOutput, calls=%fused_computation.8 | convolution fusion | flops 135528448 | bytes 2646016 | tf_op jit(solution)/shard_map/hts,shd->thd/dot_general | solution.py:38
  40.0 47.9 %all-gather.4.cloned.1.call-done = bf16[128,128,128]{2,1,0:T(8,128)(2,1)} async-done(((bf16[16,128,128]{2,1,0:T(8,128)(2,1)}), bf16[128,128,128]{2,1,0:T(8,128)(2,1)}) %all-gather.4.cloned.1.call-update) | async-done | bytes 4194320 | tf_op jit(solution)/shard_map/all_gather | solution.py:10
  87.9 10.7 %while.16 = (s32[]{:T(128)}, f32[16]{0:T(128)S(1)}, f32[16,128,128]{2,1,0:T(8,128)S(1)}, s32[]{:T(128)}, bf16[8,16]{1,0:T(8,128)(2,1)S(1)}, /*index=5*/bf16[8,16,128,128]{3,2,1,0:T(8,128)(2,1)}, s32[]{:T(128)}, s32[]{:T(128)}) while((s32[]{:T(128)}, f32[16]{0:T(128)S(1)}, f32[16,128,128]{2,1,0:T(8,128)S(1)}, s32[]{:T(128)}, ...), condition=%wide.region_2.3_spmd.clone, body=%wide.region_1.2_spmd.clone.sunk | while | flops 1310788 | bytes 2621843 | solution.py:23
  87.9 1.3 %fusion.32 = f32[16,128,128]{2,1,0:T(8,128)S(1)} fusion(f32[16,128,128]{2,1,0:T(8,128)S(1)} %get-tuple-element.207, bf16[8,16,128,128]{3,2,1,0:T(8,128)(2,1)} %get-tuple-element.218, s32[]{:T(128)} %get-tuple-element.205, f32[16]{0:T(128)S(1)} %get-tuple-element.196, pred[]{:T(512)S(6)} %compare.3, pred[]{:T(512)S(6)} %lt.22), kind=kLoop, calls=%fused_computation.1.clone.1 | loop fusion | flops 1310720 | bytes 2621510 | tf_op jit(solution)/shard_map/while/body/eval_jaxpr/jit(_where)/select_n | solution.py:21
  89.3 1.3 %fusion.32 = f32[16,128,128]{2,1,0:T(8,128)S(1)} fusion(f32[16,128,128]{2,1,0:T(8,128)S(1)} %get-tuple-element.207, bf16[8,16,128,128]{3,2,1,0:T(8,128)(2,1)} %get-tuple-element.218, s32[]{:T(128)} %get-tuple-element.205, f32[16]{0:T(128)S(1)} %get-tuple-element.196, pred[]{:T(512)S(6)} %compare.3, pred[]{:T(512)S(6)} %lt.22), kind=kLoop, calls=%fused_computation.1.clone.1 | loop fusion | flops 1310720 | bytes 2621510 | tf_op jit(solution)/shard_map/while/body/eval_jaxpr/jit(_where)/select_n | solution.py:21
  90.6 1.3 %fusion.32 = f32[16,128,128]{2,1,0:T(8,128)S(1)} fusion(f32[16,128,128]{2,1,0:T(8,128)S(1)} %get-tuple-element.207, bf16[8,16,128,128]{3,2,1,0:T(8,128)(2,1)} %get-tuple-element.218, s32[]{:T(128)} %get-tuple-element.205, f32[16]{0:T(128)S(1)} %get-tuple-element.196, pred[]{:T(512)S(6)} %compare.3, pred[]{:T(512)S(6)} %lt.22), kind=kLoop, calls=%fused_computation.1.clone.1 | loop fusion | flops 1310720 | bytes 2621510 | tf_op jit(solution)/shard_map/while/body/eval_jaxpr/jit(_where)/select_n | solution.py:21
  91.9 1.3 %fusion.32 = f32[16,128,128]{2,1,0:T(8,128)S(1)} fusion(f32[16,128,128]{2,1,0:T(8,128)S(1)} %get-tuple-element.207, bf16[8,16,128,128]{3,2,1,0:T(8,128)(2,1)} %get-tuple-element.218, s32[]{:T(128)} %get-tuple-element.205, f32[16]{0:T(128)S(1)} %get-tuple-element.196, pred[]{:T(512)S(6)} %compare.3, pred[]{:T(512)S(6)} %lt.22), kind=kLoop, calls=%fused_computation.1.clone.1 | loop fusion | flops 1310720 | bytes 2621510 | tf_op jit(solution)/shard_map/while/body/eval_jaxpr/jit(_where)/select_n | solution.py:21
  93.3 1.3 %fusion.32 = f32[16,128,128]{2,1,0:T(8,128)S(1)} fusion(f32[16,128,128]{2,1,0:T(8,128)S(1)} %get-tuple-element.207, bf16[8,16,128,128]{3,2,1,0:T(8,128)(2,1)} %get-tuple-element.218, s32[]{:T(128)} %get-tuple-element.205, f32[16]{0:T(128)S(1)} %get-tuple-element.196, pred[]{:T(512)S(6)} %compare.3, pred[]{:T(512)S(6)} %lt.22), kind=kLoop, calls=%fused_computation.1.clone.1 | loop fusion | flops 1310720 | bytes 2621510 | tf_op jit(solution)/shard_map/while/body/eval_jaxpr/jit(_where)/select_n | solution.py:21
  94.6 1.3 %fusion.32 = f32[16,128,128]{2,1,0:T(8,128)S(1)} fusion(f32[16,128,128]{2,1,0:T(8,128)S(1)} %get-tuple-element.207, bf16[8,16,128,128]{3,2,1,0:T(8,128)(2,1)} %get-tuple-element.218, s32[]{:T(128)} %get-tuple-element.205, f32[16]{0:T(128)S(1)} %get-tuple-element.196, pred[]{:T(512)S(6)} %compare.3, pred[]{:T(512)S(6)} %lt.22), kind=kLoop, calls=%fused_computation.1.clone.1 | loop fusion | flops 1310720 | bytes 2621510 | tf_op jit(solution)/shard_map/while/body/eval_jaxpr/jit(_where)/select_n | solution.py:21
  96.0 1.3 %fusion.32 = f32[16,128,128]{2,1,0:T(8,128)S(1)} fusion(f32[16,128,128]{2,1,0:T(8,128)S(1)} %get-tuple-element.207, bf16[8,16,128,128]{3,2,1,0:T(8,128)(2,1)} %get-tuple-element.218, s32[]{:T(128)} %get-tuple-element.205, f32[16]{0:T(128)S(1)} %get-tuple-element.196, pred[]{:T(512)S(6)} %compare.3, pred[]{:T(512)S(6)} %lt.22), kind=kLoop, calls=%fused_computation.1.clone.1 | loop fusion | flops 1310720 | bytes 2621510 | tf_op jit(solution)/shard_map/while/body/eval_jaxpr/jit(_where)/select_n | solution.py:21
  97.3 1.3 %fusion.32 = f32[16,128,128]{2,1,0:T(8,128)S(1)} fusion(f32[16,128,128]{2,1,0:T(8,128)S(1)} %get-tuple-element.207, bf16[8,16,128,128]{3,2,1,0:T(8,128)(2,1)} %get-tuple-element.218, s32[]{:T(128)} %get-tuple-element.205, f32[16]{0:T(128)S(1)} %get-tuple-element.196, pred[]{:T(512)S(6)} %compare.3, pred[]{:T(512)S(6)} %lt.22), kind=kLoop, calls=%fused_computation.1.clone.1 | loop fusion | flops 1310720 | bytes 2621510 | tf_op jit(solution)/shard_map/while/body/eval_jaxpr/jit(_where)/select_n | solution.py:21
  98.6 0.0 copy-start.2
  98.6 0.0 copy-done.1
  98.6 2.1 %multiply_reduce_fusion = (f32[128]{0:T(128)S(1)}, f32[128,16,128]{0,2,1:T(8,128)S(1)}) fusion(f32[128,16,128]{0,2,1:T(8,128)} %convolution_bitcast_fusion.1, f32[128,16]{0,1:T(8,128)S(1)} %get-tuple-element.152, f32[16,128,128]{2,1,0:T(8,128)S(1)} %get-tuple-element.116, bf16[16,128,128]{2,1,0:T(8,128)(2,1)S(1)} %copy-done.1, f32[16]{0:T(128)S(1)} %exp.34, ...), kind=kOutput, calls=%fused_computation.13 | convolution fusion | flops 69730176 | bytes 4203072 | tf_op jit(solution)/shard_map/thd,hde->the/dot_general | solution.py:67
  100.7 0.3 copy.26
  101.1 2.5 %psum.7 = f32[128]{0:T(128)S(1)} all-reduce(f32[128]{0:T(128)S(1)} %get-tuple-element.154), channel_id=1, replica_groups=mesh['groups'=2,'seq'=8,'tp'=2] {'tp'}, use_global_device_ids=true, to_apply=%region_4.5 | all-reduce | flops 128 | bytes 1024 | tf_op jit(solution)/shard_map/psum | solution.py:71
  103.6 0.0 copy-done.2
  103.6 1.0 multiply_convert_fusion
  (15 shorter events, 0.2 us)
Async XLA Ops:
  6.5 30.7 %copy-start = (bf16[128,2048]{1,0:T(8,128)(2,1)S(1)}, bf16[128,2048]{1,0:T(8,128)(2,1)}, u32[]{:S(2)}) copy-start(bf16[128,2048]{1,0:T(8,128)(2,1)} %param.8) | copy-start | bytes 1572868
  6.5 81.3 %all-gather.4.cloned.1.call-start = ((), (), s32[]{:S(2)}) async-start(), calls=%async_computation | async-start | bytes 4718592 | tf_op jit(solution)/shard_map/all_gather | solution.py:10
  87.9 10.8 %copy-start.1 = (bf16[16,128,128]{2,1,0:T(8,128)(2,1)S(1)}, bf16[16,128,128]{2,1,0:T(8,128)(2,1)}, u32[]{:S(2)}) copy-start(bf16[16,128,128]{2,1,0:T(8,128)(2,1)} %param.12) | copy-start | bytes 1572868
  98.6 5.0 %copy-start.2 = (f32[2048]{0:T(1024)S(1)}, f32[2048]{0:T(1024)}, u32[]{:S(2)}) copy-start(f32[2048]{0:T(1024)} %param.13) | copy-start | bytes 24580
Sparse Core Ops, SparseCore 0:
  11.5 76.3 all-gather.3
where the time goes:
time: 112 us; the launch traced here: 111 us
  waiting for transfers between devices  47.9 us (43%)
  blocking collectives  25.9 us (23%)
  between operations  14.1 us (13%)
  other arithmetic  12.6 us (11%)
  matrix products  7.01 us (6%)
  local copies, waits for them, and re-layouts  3.63 us (3%)
    all_gather x1, waiting for transfers between devices, prefix(): lax.all_gather(part.astype(kind), axis)  47.9 us
    unnamed x1, blocking collectives  23.4 us
    select_n x8, other arithmetic, step(): return jax.tree.map(lambda a, b: jnp.where(reached, a, b), new, before)  10.4 us
    dot_general x1, matrix products, block_local(): jnp.einsum('hts,shd->thd', mixing, value_heads, preferred_element_type=jn...  2.75 us
    psum x1, blocking collectives, per_device(): square_total = lax.psum(jnp.sum(combined * combined, axis=1), 'tp')  2.47 us
  transfers between devices with their start and end apart: 1, of which 1 were waited for; matrix products, arithmetic and copies ran while one was open for 4% of the time, Pallas kernels for 0%

commit v1 on v0

v1 whole, which is shorter than its diff:
```python
import functools

import jax
import jax.numpy as jnp
from jax import lax
from jax.experimental import pallas as pl
from jax.experimental.pallas import tpu as pltpu
from jax.sharding import PartitionSpec as P

MESH = pl.DeviceIdType.MESH
F32 = jnp.float32
BF16 = jnp.bfloat16
EXACT = lax.Precision.HIGHEST


def kernel(
    pairs,
    features,
    query_hbm,
    key_hbm,
    value_hbm,
    decay_ref,
    carried_hbm,
    gain_ref,
    out_ref,
    query,
    key,
    value,
    state_out,
    state_in,
    own_state,
    sums,
    chain_out,
    chain_in,
    enter_out,
    enter_in,
    logs_out,
    logs_in,
    combined,
    squares_out,
    squares_in,
    load_sem,
    state_send,
    state_recv,
    chain_send,
    chain_recv,
    enter_send,
    enter_recv,
    small_send,
    small_recv,
):
    heads, tokens = decay_ref.shape
    half = heads // 2
    width = query.shape[1] // heads
    seq = lax.axis_index("seq")
    tp = lax.axis_index("tp")
    side = lax.rem(seq, 2)
    pair = lax.div(seq, 2)
    partner = seq + 1 - 2 * side
    first = side == 0
    not_start = jnp.where(pair > 0, 1, 0)
    not_end = jnp.where(pair < pairs - 1, 1, 0)

    loads = [
        pltpu.make_async_copy(key_hbm, key, load_sem.at[0]),
        pltpu.make_async_copy(value_hbm, value, load_sem.at[1]),
        pltpu.make_async_copy(query_hbm, query, load_sem.at[2]),
    ]
    for load in loads:
        load.start()

    barrier = pltpu.get_barrier_semaphore()
    pl.semaphore_signal(barrier, inc=1, device_id={"seq": partner}, device_id_type=MESH)
    pl.semaphore_signal(barrier, inc=1, device_id={"tp": 1 - tp}, device_id_type=MESH)

    @pl.when(pair > 0)
    def _():
        pl.semaphore_signal(barrier, inc=1, device_id={"seq": seq - 2}, device_id_type=MESH)

    @pl.when(pair < pairs - 1)
    def _():
        pl.semaphore_signal(barrier, inc=1, device_id={"seq": seq + 2}, device_id_type=MESH)

    direct = chain_in.dtype == carried_hbm.dtype
    carried_copy = pltpu.make_async_copy(
        carried_hbm.at[pl.ds(side * half, half)], chain_in if direct else sums, load_sem.at[3]
    )

    @pl.when(pair == 0)
    def _():
        carried_copy.start()

    decay = decay_ref[...]
    decay = jnp.where(first, decay, jnp.concatenate([decay[half:], decay[:half]], axis=0))
    t_index = lax.broadcasted_iota(jnp.int32, (tokens, tokens), 0)
    s_index = lax.broadcasted_iota(jnp.int32, (tokens, tokens), 1)
    causal = s_index <= t_index
    lower = jnp.where(causal, 1.0, 0.0).astype(F32)
    contract_last = (((1,), (1,)), ((), ()))
    cumul_row = lax.dot_general(decay, lower, contract_last, precision=EXACT, preferred_element_type=F32)
    cumul_col = lax.dot_general(lower, decay, contract_last, precision=EXACT, preferred_element_type=F32)
    after_col = lax.dot_general(
        1.0 - lower, decay, contract_last, precision=EXACT, preferred_element_type=F32
    )
    total = jnp.dot(
        decay, jnp.ones((tokens, width), F32), precision=EXACT, preferred_element_type=F32
    )
    key_scale = jnp.exp(after_col)
    query_scale = jnp.exp(cumul_col)
    logs_out[...] = total

    def columns(i):
        head = lax.rem(side * half + i, heads)
        return pl.ds(pl.multiple_of(head * width, width), width)

    def send(src, dst, send_sem, recv_sem, where):
        return pltpu.make_async_remote_copy(
            src_ref=src,
            dst_ref=dst,
            send_sem=send_sem,
            recv_sem=recv_sem,
            device_id=where,
            device_id_type=MESH,
        )

    logs_copy = send(logs_out, logs_in, small_send.at[0], small_recv.at[0], {"seq": partner})
    squares_copy = send(
        squares_out, squares_in, small_send.at[1], small_recv.at[1], {"tp": 1 - tp}
    )
    state_copy = [
        send(state_out.at[i], state_in.at[i], state_send.at[i], state_recv.at[i], {"seq": partner})
        for i in range(half)
    ]
    chain_copy = [
        send(chain_out.at[i], chain_in.at[i], chain_send.at[i], chain_recv.at[i], {"seq": seq + 2})
        for i in range(half)
    ]
    enter_copy = [
        send(enter_out.at[i], enter_in.at[i], enter_send.at[i], enter_recv.at[i], {"seq": partner})
        for i in range(half)
    ]

    def block_state(i):
        at = columns(i)
        decayed = (key[:, at].astype(F32) * key_scale[:, i : i + 1]).astype(BF16)
        return lax.dot_general(
            decayed, value[:, at], (((0,), (0,)), ((), ())), preferred_element_type=F32
        ).astype(BF16)

    def mixing(i):
        at = columns(i)
        scores = lax.dot_general(
            query[:, at], key[:, at], contract_last, preferred_element_type=F32
        )
        spread = cumul_col[:, i : i + 1] - cumul_row[i : i + 1, :]
        weights = jnp.where(causal, jnp.exp(jnp.minimum(spread, 0.0)), 0.0)
        return (scores * weights).astype(BF16)

    def attend(i, mixed, entering):
        at = columns(i)
        decayed = (query[:, at].astype(F32) * query_scale[:, i : i + 1]).astype(BF16)
        left = jnp.concatenate([mixed, decayed], axis=1)
        right = jnp.concatenate([value[:, at], entering], axis=0)
        result = jnp.dot(left, right, preferred_element_type=F32)
        combined[:, at] = result
        return result * result

    pl.semaphore_wait(barrier, 2 + not_start + not_end)
    logs_copy.start()
    loads[0].wait()
    loads[1].wait()
    for i in range(half):
        state_out[i] = block_state(half + i)
        state_copy[i].start()
    for i in range(half):
        own_state[i] = block_state(i)
    loads[2].wait()
    logs_copy.wait_recv()

    @pl.when(pair == 0)
    def _():
        carried_copy.wait()
        if not direct:
            chain_in[...] = sums[...].astype(chain_in.dtype)

    own_log = total[:half]
    other_log = logs_in[half:, :]
    first_decay = jnp.exp(jnp.where(first, own_log, other_log))
    second_decay = jnp.exp(jnp.where(first, other_log, own_log))
    both_decay = jnp.exp(own_log + other_log)

    squares = jnp.zeros((tokens, width), F32)
    for i in range(half):
        state_copy[i].wait_recv()
        mine = own_state[i].astype(F32)
        theirs = state_in[i].astype(F32)
        state_first = jnp.where(first, mine, theirs)
        state_second = jnp.where(first, theirs, mine)
        both = second_decay[i : i + 1] * state_first + state_second

        @pl.when(pair > 0)
        def _():
            chain_copy[i].wait_recv()

        before = chain_in[i].astype(F32)
        chain_out[i] = (both_decay[i : i + 1] * before + both).astype(chain_out.dtype)

        @pl.when(pair < pairs - 1)
        def _():
            chain_copy[i].start()

        between = first_decay[i : i + 1] * before + state_first
        enter_out[i] = jnp.where(first, between, before).astype(BF16)
        enter_copy[i].start()
        entering = jnp.where(first, before, between).astype(BF16)
        squares = squares + attend(i, mixing(i), entering)
    for i in range(half):
        mixed = mixing(half + i)
        enter_copy[i].wait_recv()
        squares = squares + attend(half + i, mixed, enter_in[i])

    squares_out[...] = squares
    squares_copy.start()
    squares_copy.wait_recv()
    meansq = jnp.sum(squares + squares_in[...], axis=1, keepdims=True) / features
    scale = lax.rsqrt(meansq + 1e-06)
    for i in range(heads):
        at = slice(i * width, (i + 1) * width)
        out_ref[:, at] = (combined[:, at] * scale * gain_ref[:, at]).astype(BF16)

    logs_copy.wait_send()
    squares_copy.wait_send()
    for i in range(half):
        state_copy[i].wait_send()
        enter_copy[i].wait_send()

    @pl.when(pair < pairs - 1)
    def _():
        for i in range(half):
            chain_copy[i].wait_send()


def per_device(query_rows, key_rows, value_rows, log_decay, carried_state, norm_gain):
    tokens, columns = query_rows.shape
    heads, depth, width = carried_state.shape
    half = heads // 2
    devices = lax.axis_size("seq")
    chain_dtype = BF16 if devices <= 16 else F32
    block = (half, depth, width)
    vmem = pl.BlockSpec(memory_space=pltpu.VMEM)
    hbm = pl.BlockSpec(memory_space=pl.ANY)
    dma = pltpu.SemaphoreType.DMA
    return pl.pallas_call(
        functools.partial(kernel, devices // 2, columns * lax.axis_size("tp")),
        out_shape=jax.ShapeDtypeStruct((tokens, columns), BF16),
        in_specs=[hbm, hbm, hbm, vmem, hbm, vmem],
        out_specs=vmem,
        scratch_shapes=[
            pltpu.VMEM((tokens, columns), BF16),
            pltpu.VMEM((tokens, columns), BF16),
            pltpu.VMEM((tokens, columns), BF16),
            pltpu.VMEM(block, BF16),
            pltpu.VMEM(block, BF16),
            pltpu.VMEM(block, BF16),
            pltpu.VMEM(block, BF16),
            pltpu.VMEM(block, chain_dtype),
            pltpu.VMEM(block, chain_dtype),
            pltpu.VMEM(block, BF16),
            pltpu.VMEM(block, BF16),
            pltpu.VMEM((heads, width), F32),
            pltpu.VMEM((heads, width), F32),
            pltpu.VMEM((tokens, columns), F32),
            pltpu.VMEM((tokens, width), F32),
            pltpu.VMEM((tokens, width), F32),
            dma((4,)),
            dma((half,)),
            dma((half,)),
            dma((half,)),
            dma((half,)),
            dma((half,)),
            dma((half,)),
            dma((2,)),
            dma((2,)),
        ],
        compiler_params=pltpu.CompilerParams(
            collective_id=0, has_side_effects=True, vmem_limit_bytes=63 * 1024 * 1024
        ),
    )(query_rows, key_rows, value_rows, log_decay, carried_state, norm_gain.reshape(1, columns))


def solution(mesh):
    in_specs = (
        P(("groups", "seq"), "tp"),
        P(("groups", "seq"), "tp"),
        P(("groups", "seq"), "tp"),
        P("tp", ("groups", "seq")),
        P(("groups", "tp"), None, None),
        P("tp"),
    )
    return jax.shard_map(
        per_device,
        mesh=mesh,
        in_specs=in_specs,
        out_specs=P(("groups", "seq"), "tp"),
        check_vma=False,
    )
```

time: 112 us -> 26 us (0.23)
  the two profiles are of different devices: /device:TPU:0 before, /device:TPU:31 now
where the time goes in v1:
time: 26 us; the launch traced here: 25.8 us
  Pallas kernels  23.9 us (92%)
  local copies, waits for them, and re-layouts  1.88 us (7%)
    pallas_call x1, Pallas kernels, per_device(): pl.pallas_call(functools.partial(kernel, devices // 2, columns * lax.axis...  23.9 us
    unnamed x1, local copies, waits for them, and re-layouts  1.88 us

profile of v1, /device:TPU:31, one launch (start us, length us, event | category | flops | bytes accessed | tf_op | source)
XLA Modules:
  0.0 25.8 jit_solution(3622594094221701408)
XLA Ops:
  0.0 23.9 %shard_map.64 = bf16[128,2048]{1,0:T(8,128)(2,1)} custom-call(bf16[128,2048]{1,0:T(8,128)(2,1)} %query_hbm.1, bf16[128,2048]{1,0:T(8,128)(2,1)} %key_hbm.1, bf16[128,2048]{1,0:T(8,128)(2,1)} %value_hbm.1, f32[16,128]{1,0:T(8,128)} %decay_ref.1, bf16[16,128,128]{2,1,0:T(8,128)(2,1)} %carried_hbm.1, f32[1,2048]{1,0:T(1,128)} %bitcast.1), custom_call_target="tpu_custom_call" | custom-call | tf_op jit(solution)/shard_map/pallas_call | solution.py:253
  23.9 1.9 %copy.8 = bf16[128,2048]{1,0:T(8,128)(2,1)} copy(bf16[128,2048]{1,0:T(8,128)(2,1)} %shard_map.64) | data formatting | bytes 1048576

commit v2 on v1

--- a/solution.py
+++ b/solution.py
@@ -19,13 +19,15 @@
     query_hbm,
     key_hbm,
     value_hbm,
-    decay_ref,
+    decay_hbm,
     carried_hbm,
-    gain_ref,
+    gain_hbm,
     out_ref,
     query,
     key,
     value,
+    decay_ref,
+    gain_ref,
     state_out,
     state_in,
     own_state,
@@ -61,26 +63,29 @@
     not_start = jnp.where(pair > 0, 1, 0)
     not_end = jnp.where(pair < pairs - 1, 1, 0)
 
+    barrier = pltpu.get_barrier_semaphore()
+    pl.semaphore_signal(barrier, inc=1, device_id={"seq": partner}, device_id_type=MESH)
+    pl.semaphore_signal(barrier, inc=1, device_id={"tp": 1 - tp}, device_id_type=MESH)
+
+    @pl.when(pair > 0)
+    def _():
+        pl.semaphore_signal(barrier, inc=1, device_id={"seq": seq - 2}, device_id_type=MESH)
+
+    @pl.when(pair < pairs - 1)
+    def _():
+        pl.semaphore_signal(barrier, inc=1, device_id={"seq": seq + 2}, device_id_type=MESH)
+
+    decay_load = pltpu.make_async_copy(decay_hbm, decay_ref, load_sem.at[5])
+    decay_load.start()
     loads = [
         pltpu.make_async_copy(key_hbm, key, load_sem.at[0]),
         pltpu.make_async_copy(value_hbm, value, load_sem.at[1]),
         pltpu.make_async_copy(query_hbm, query, load_sem.at[2]),
+        pltpu.make_async_copy(gain_hbm, gain_ref, load_sem.at[4]),
     ]
     for load in loads:
         load.start()
 
-    barrier = pltpu.get_barrier_semaphore()
-    pl.semaphore_signal(barrier, inc=1, device_id={"seq": partner}, device_id_type=MESH)
-    pl.semaphore_signal(barrier, inc=1, device_id={"tp": 1 - tp}, device_id_type=MESH)
-
-    @pl.when(pair > 0)
-    def _():
-        pl.semaphore_signal(barrier, inc=1, device_id={"seq": seq - 2}, device_id_type=MESH)
-
-    @pl.when(pair < pairs - 1)
-    def _():
-        pl.semaphore_signal(barrier, inc=1, device_id={"seq": seq + 2}, device_id_type=MESH)
-
     direct = chain_in.dtype == carried_hbm.dtype
     carried_copy = pltpu.make_async_copy(
         carried_hbm.at[pl.ds(side * half, half)], chain_in if direct else sums, load_sem.at[3]
@@ -90,6 +95,7 @@
     def _():
         carried_copy.start()
 
+    decay_load.wait()
     decay = decay_ref[...]
     decay = jnp.where(first, decay, jnp.concatenate([decay[half:], decay[:half]], axis=0))
     t_index = lax.broadcasted_iota(jnp.int32, (tokens, tokens), 0)
@@ -211,9 +217,19 @@
 
         between = first_decay[i : i + 1] * before + state_first
         enter_out[i] = jnp.where(first, between, before).astype(BF16)
-        enter_copy[i].start()
+
+        @pl.when(pair > 0)
+        def _():
+            enter_copy[i].start()
+
         entering = jnp.where(first, before, between).astype(BF16)
         squares = squares + attend(i, mixing(i), entering)
+
+    @pl.when(pair == 0)
+    def _():
+        for i in range(half):
+            enter_copy[i].start()
+
     for i in range(half):
         mixed = mixing(half + i)
         enter_copy[i].wait_recv()
@@ -222,6 +238,7 @@
     squares_out[...] = squares
     squares_copy.start()
     squares_copy.wait_recv()
+    loads[3].wait()
     meansq = jnp.sum(squares + squares_in[...], axis=1, keepdims=True) / features
     scale = lax.rsqrt(meansq + 1e-06)
     for i in range(heads):
@@ -252,13 +269,15 @@
     dma = pltpu.SemaphoreType.DMA
     return pl.pallas_call(
         functools.partial(kernel, devices // 2, columns * lax.axis_size("tp")),
-        out_shape=jax.ShapeDtypeStruct((tokens, columns), BF16),
-        in_specs=[hbm, hbm, hbm, vmem, hbm, vmem],
+        out_shape=pltpu.VMEM((tokens, columns), BF16),
+        in_specs=[hbm] * 6,
         out_specs=vmem,
         scratch_shapes=[
             pltpu.VMEM((tokens, columns), BF16),
             pltpu.VMEM((tokens, columns), BF16),
             pltpu.VMEM((tokens, columns), BF16),
+            pltpu.VMEM((heads, tokens), F32),
+            pltpu.VMEM((1, columns), F32),
             pltpu.VMEM(block, BF16),
             pltpu.VMEM(block, BF16),
             pltpu.VMEM(block, BF16),
@@ -272,7 +291,7 @@
             pltpu.VMEM((tokens, columns), F32),
             pltpu.VMEM((tokens, width), F32),
             pltpu.VMEM((tokens, width), F32),
-            dma((4,)),
+            dma((6,)),
             dma((half,)),
             dma((half,)),
             dma((half,)),
@@ -283,7 +302,7 @@
             dma((2,)),
         ],
         compiler_params=pltpu.CompilerParams(
-            collective_id=0, has_side_effects=True, vmem_limit_bytes=63 * 1024 * 1024
+            collective_id=0, has_side_effects=True, vmem_limit_bytes=56 * 1024 * 1024
         ),
     )(query_rows, key_rows, value_rows, log_decay, carried_state, norm_gain.reshape(1, columns))
 

time: 26 us -> 22.3 us (0.86)
  Pallas kernels: 23.9 us -> 21.3 us
  local copies, waits for them, and re-layouts: 1.88 us -> 0.8 us
    pallas_call x1, Pallas kernels: 23.9 us -> 21.3 us  [per_device(): pl.pallas_call(functools.partial(kernel, devices // 2, columns * lax.axis...]
    unnamed x1, local copies, waits for them, and re-layouts: 1.88 us -> 0.8 us
where the time goes in v2:
time: 22.3 us; the launch traced here: 22.1 us
  Pallas kernels  21.3 us (96%)
  local copies, waits for them, and re-layouts  0.8 us (4%)
    pallas_call x1, Pallas kernels, per_device(): pl.pallas_call(functools.partial(kernel, devices // 2, columns * lax.axis...  21.3 us
    unnamed x1, local copies, waits for them, and re-layouts  0.8 us

profile of v2, /device:TPU:31, one launch (start us, length us, event | category | flops | bytes accessed | tf_op | source)
XLA Modules:
  0.0 22.1 jit_solution(8376179112100043548)
XLA Ops:
  0.0 21.3 %shard_map.64 = bf16[128,2048]{1,0:T(8,128)(2,1)S(1)} custom-call(bf16[128,2048]{1,0:T(8,128)(2,1)} %query_hbm.1, bf16[128,2048]{1,0:T(8,128)(2,1)} %key_hbm.1, bf16[128,2048]{1,0:T(8,128)(2,1)} %value_hbm.1, f32[16,128]{1,0:T(8,128)} %decay_hbm.1, bf16[16,128,128]{2,1,0:T(8,128)(2,1)} %carried_hbm.1, f32[1,2048]{1,0:T(1,128)} %bitcast.1), custom_call_target="tpu_custom_call" | custom-call | tf_op jit(solution)/shard_map/pallas_call | solution.py:270
  21.3 0.8 %copy.8 = bf16[128,2048]{1,0:T(8,128)(2,1)} copy(bf16[128,2048]{1,0:T(8,128)(2,1)S(1)} %shard_map.64) | data formatting | bytes 1048576

commit v3 on v2

--- a/solution.py
+++ b/solution.py
@@ -10,6 +10,7 @@
 MESH = pl.DeviceIdType.MESH
 F32 = jnp.float32
 BF16 = jnp.bfloat16
+EARLY = 2
 EXACT = lax.Precision.HIGHEST
 
 
@@ -36,6 +37,7 @@
     chain_in,
     enter_out,
     enter_in,
+    mixed,
     logs_out,
     logs_in,
     combined,
@@ -162,13 +164,13 @@
         weights = jnp.where(causal, jnp.exp(jnp.minimum(spread, 0.0)), 0.0)
         return (scores * weights).astype(BF16)
 
-    def attend(i, mixed, entering):
+    def attend(i, entering):
         at = columns(i)
         decayed = (query[:, at].astype(F32) * query_scale[:, i : i + 1]).astype(BF16)
-        left = jnp.concatenate([mixed, decayed], axis=1)
+        left = jnp.concatenate([mixed[i], decayed], axis=1)
         right = jnp.concatenate([value[:, at], entering], axis=0)
         result = jnp.dot(left, right, preferred_element_type=F32)
-        combined[:, at] = result
+        combined[:, at] = result * gain_ref[:, at]
         return result * result
 
     pl.semaphore_wait(barrier, 2 + not_start + not_end)
@@ -181,6 +183,7 @@
     for i in range(half):
         own_state[i] = block_state(i)
     loads[2].wait()
+    loads[3].wait()
     logs_copy.wait_recv()
 
     @pl.when(pair == 0)
@@ -188,6 +191,11 @@
         carried_copy.wait()
         if not direct:
             chain_in[...] = sums[...].astype(chain_in.dtype)
+
+    @pl.when(pair >= EARLY)
+    def _():
+        for i in range(heads):
+            mixed[i] = mixing(i)
 
     own_log = total[:half]
     other_log = logs_in[half:, :]
@@ -222,28 +230,32 @@
         def _():
             enter_copy[i].start()
 
-        entering = jnp.where(first, before, between).astype(BF16)
-        squares = squares + attend(i, mixing(i), entering)
+        own_state[i] = jnp.where(first, before, between).astype(BF16)
 
     @pl.when(pair == 0)
     def _():
         for i in range(half):
             enter_copy[i].start()
 
-    for i in range(half):
-        mixed = mixing(half + i)
+    @pl.when(pair < EARLY)
+    def _():
+        for i in range(heads):
+            mixed[i] = mixing(i)
+
+    for i in range(half):
+        squares = squares + attend(i, own_state[i])
+    for i in range(half):
         enter_copy[i].wait_recv()
-        squares = squares + attend(half + i, mixed, enter_in[i])
+        squares = squares + attend(half + i, enter_in[i])
 
     squares_out[...] = squares
     squares_copy.start()
     squares_copy.wait_recv()
-    loads[3].wait()
     meansq = jnp.sum(squares + squares_in[...], axis=1, keepdims=True) / features
     scale = lax.rsqrt(meansq + 1e-06)
     for i in range(heads):
         at = slice(i * width, (i + 1) * width)
-        out_ref[:, at] = (combined[:, at] * scale * gain_ref[:, at]).astype(BF16)
+        out_ref[:, at] = (combined[:, at] * scale).astype(BF16)
 
     logs_copy.wait_send()
     squares_copy.wait_send()
@@ -286,6 +298,7 @@
             pltpu.VMEM(block, chain_dtype),
             pltpu.VMEM(block, BF16),
             pltpu.VMEM(block, BF16),
+            pltpu.VMEM((heads, tokens, tokens), BF16),
             pltpu.VMEM((heads, width), F32),
             pltpu.VMEM((heads, width), F32),
             pltpu.VMEM((tokens, columns), F32),

time: 22.3 us -> 22.3 us (level)
  no operation moved by 1% of the time
where the time goes in v3:
time: 22.3 us; the launch traced here: 22.1 us
  Pallas kernels  21.3 us (96%)
  local copies, waits for them, and re-layouts  0.8 us (4%)
    pallas_call x1, Pallas kernels, per_device(): pl.pallas_call(functools.partial(kernel, devices // 2, columns * lax.axis...  21.3 us
    unnamed x1, local copies, waits for them, and re-layouts  0.8 us

profile of v3, /device:TPU:31, one launch (start us, length us, event | category | flops | bytes accessed | tf_op | source)
XLA Modules:
  0.0 22.1 jit_solution(174304229313284043)
XLA Ops:
  0.0 21.3 %shard_map.64 = bf16[128,2048]{1,0:T(8,128)(2,1)S(1)} custom-call(bf16[128,2048]{1,0:T(8,128)(2,1)} %query_hbm.1, bf16[128,2048]{1,0:T(8,128)(2,1)} %key_hbm.1, bf16[128,2048]{1,0:T(8,128)(2,1)} %value_hbm.1, f32[16,128]{1,0:T(8,128)} %decay_hbm.1, bf16[16,128,128]{2,1,0:T(8,128)(2,1)} %carried_hbm.1, f32[1,2048]{1,0:T(1,128)} %bitcast.1), custom_call_target="tpu_custom_call" | custom-call | tf_op jit(solution)/shard_map/pallas_call | solution.py:282
  21.3 0.8 %copy.8 = bf16[128,2048]{1,0:T(8,128)(2,1)} copy(bf16[128,2048]{1,0:T(8,128)(2,1)S(1)} %shard_map.64) | data formatting | bytes 1048576
